TPU v7x, 32 devices: a whole 2x2x4 slice. The times are simulated.
32 devices in a mesh: srow: 4 (over z), scol: 4 (over x, core), trow: 2 (over y).
Axes of the slice: x: 2, y: 2, z: 4, core: 2. Of those that a mesh axis runs over, the one named last changes fastest.
Arguments:
- volume: bfloat16 [8, 8, 16, 128, 128], P(None, 'srow', 'scol', 'trow'), may hold values from -6 to 6
- src_weight: bfloat16 [2, 9, 8, 8], replicated, may hold values from -0.75 to 0.75
- tgt_weight: bfloat16 [2, 9, 8, 8], replicated, may hold values from -0.75 to 0.75
- bias: float32 [2, 8], replicated, may hold values from -3 to 3
Outputs:
- refined: bfloat16 [8, 8, 16, 128, 128], P(None, 'srow', 'scol', 'trow')
All inputs are finite; a program needn't handle non-finite values.
Results may differ from a plain program's by a relative error of at most 0.0036.
Values may be sent and summed in bfloat16 or wider, within the bound.
No kernel may reach another device: no remote copies, remote signals or barrier semaphores. Data moves between devices by JAX's collectives and lax.ppermute only.
A program may use at most 64 MiB of HBM per device.

v0:
```python
import jax
import jax.numpy as jnp
from jax import lax
from jax.sharding import PartitionSpec as P


def padded(block, sides, width):
    for axis, dim in sides:
        count = lax.axis_size(axis)
        forward = [(i, i + 1) for i in range(count - 1)]
        backward = [(target, source) for source, target in forward]
        low = lax.ppermute(
            lax.slice_in_dim(block, block.shape[dim] - width, None, axis=dim), axis, forward
        )
        high = lax.ppermute(lax.slice_in_dim(block, 0, width, axis=dim), axis, backward)
        block = jnp.concatenate([low, block, high], axis=dim)
    return block


def apply_layer(src_pad, tgt_pad, w_src, w_tgt, bias_row):
    channels, rows_two, cols_two, depth, width = src_pad.shape
    row_count = rows_two - 2
    col_count = cols_two - 2
    widened = jnp.pad(tgt_pad, ((0, 0), (0, 0), (0, 0), (0, 0), (1, 1)))
    src_kernel = jnp.transpose(w_src, (1, 0, 2)).reshape(channels, 9 * channels)
    tgt_kernel = jnp.transpose(w_tgt, (1, 0, 2)).reshape(channels, 9 * channels)
    kernel = jnp.concatenate([src_kernel, tgt_kernel], axis=1)
    out_blocks = []
    for offset in range(0, depth, 8):
        extent = min(8, depth - offset)
        pieces = []
        for first in range(3):
            for second in range(3):
                pieces.append(
                    src_pad[
                        :,
                        first : first + row_count,
                        second : second + col_count,
                        offset : offset + extent,
                    ]
                )
        for first in range(3):
            for second in range(3):
                pieces.append(
                    widened[
                        :, :, :, offset + first : offset + first + extent, second : second + width
                    ]
                )
        stacked = jnp.concatenate(pieces, axis=0)
        total = jnp.einsum("om,mijkl->oijkl", kernel, stacked, preferred_element_type=jnp.float32)
        center = tgt_pad[:, :, :, 1 + offset : 1 + offset + extent].astype(jnp.float32)
        out_blocks.append(center + jnp.maximum(total + bias_row[:, None, None, None, None], 0.0))
    return jnp.concatenate(out_blocks, axis=3)


def shards(volume, src_weight, tgt_weight, bias):
    layer_count = src_weight.shape[0]
    state = volume
    for layer_id in range(layer_count):
        src_pad = padded(state, (("srow", 1), ("scol", 2)), 1)
        tgt_pad = padded(state, (("trow", 3),), 1)
        state = apply_layer(
            src_pad, tgt_pad, src_weight[layer_id], tgt_weight[layer_id], bias[layer_id]
        ).astype(jnp.bfloat16)
    return state


def solution(mesh):
    return jax.shard_map(
        shards,
        mesh=mesh,
        in_specs=(P(None, "srow", "scol", "trow", None), P(), P(), P()),
        out_specs=P(None, "srow", "scol", "trow", None),
        check_vma=False,
    )
```

profile of v0, /device:TPU:6, one launch (start us, length us, event | category | flops | bytes accessed | tf_op | source)
XLA Modules:
  0.0 105.1 jit_solution(6120225037858064904)
XLA Ops:
  0.0 1.9 %copy.42 = bf16[8,2,4,64,128]{4,0,3,2,1:T(8,128)(2,1)S(1)} copy(bf16[8,2,4,64,128]{4,3,2,1,0:T(8,128)(2,1)} %param.4) | data formatting | bytes 2097152 | tf_op args[0]
  2.0 3.6 %collective-permute-start = (bf16[8,1,4,64,128]{4,0,3,2,1:T(8,128)(2,1)S(1)}, bf16[8,1,4,64,128]{4,0,3,2,1:T(8,128)(2,1)S(1)}, u32[]{:S(2)}, u32[]{:S(2)}) collective-permute-start(bf16[8,1,4,64,128]{4,0,3,2,1:T(8,128)(2,1)S(1)} %get-tuple-element.248), channel_id=1, source_target_pairs={{0,8},{8,16},{16,24},{1,9},{9,17},{17,25},{2,10},{10,18},{18,26},{... | collective-permute-start | bytes 1572872 | tf_op jit(solution)/shard_map/ppermute | solution.py:12
  5.7 1.3 %collective-permute-start.4 = (bf16[8,2,4,1,128]{4,0,3,2,1:T(8,128)(2,1)S(1)}, bf16[8,2,4,1,128]{4,0,3,2,1:T(8,128)(2,1)S(1)}, u32[]{:S(2)}, u32[]{:S(2)}) collective-permute-start(bf16[8,2,4,1,128]{4,0,3,2,1:T(8,128)(2,1)S(1)} %get-tuple-element.242), channel_id=1, source_target_pairs={{0,1},{2,3},{4,5},{6,7},{8,9},{10,11},{12,13},{14,15},{16,17},{18,... | collective-permute-start | bytes 49160 | tf_op jit(solution)/shard_map/ppermute | solution.py:12
  7.0 4.5 %collective-permute-start.5 = (bf16[8,2,4,1,128]{4,0,3,2,1:T(8,128)(2,1)S(1)}, bf16[8,2,4,1,128]{4,0,3,2,1:T(8,128)(2,1)S(1)}, u32[]{:S(2)}, u32[]{:S(2)}) collective-permute-start(bf16[8,2,4,1,128]{4,0,3,2,1:T(8,128)(2,1)S(1)} %get-tuple-element.243), channel_id=1, source_target_pairs={{1,0},{3,2},{5,4},{7,6},{9,8},{11,10},{13,12},{15,14},{17,16},{19,... | collective-permute-start | bytes 49160 | tf_op jit(solution)/shard_map/ppermute | solution.py:15
  11.5 1.3 %collective-permute-start.1 = (bf16[8,1,4,64,128]{4,0,3,2,1:T(8,128)(2,1)S(1)}, bf16[8,1,4,64,128]{4,0,3,2,1:T(8,128)(2,1)S(1)}, u32[]{:S(2)}, u32[]{:S(2)}) collective-permute-start(bf16[8,1,4,64,128]{4,0,3,2,1:T(8,128)(2,1)S(1)} %get-tuple-element.247), channel_id=1, source_target_pairs={{8,0},{16,8},{24,16},{9,1},{17,9},{25,17},{10,2},{18,10},{26,18},{... | collective-permute-start | bytes 1572872 | tf_op jit(solution)/shard_map/ppermute | solution.py:15
  12.9 0.6 slice_bitcast_fusion.1
  13.5 0.6 slice_bitcast_fusion
  14.1 2.7 %collective-permute-done = bf16[8,1,4,64,128]{4,0,3,2,1:T(8,128)(2,1)S(1)} collective-permute-done((bf16[8,1,4,64,128]{4,0,3,2,1:T(8,128)(2,1)S(1)}, bf16[8,1,4,64,128]{4,0,3,2,1:T(8,128)(2,1)S(1)}, u32[]{:S(2)}, u32[]{:S(2)}) %collective-permute-start) | collective-permute-done | bytes 524320 | tf_op jit(solution)/shard_map/ppermute | solution.py:12
  17.0 1.1 %constant_dynamic-update-slice_fusion.6 = (bf16[8,3,4,64,128]{4,0,3,2,1:T(8,128)(2,1)S(1)}, bf16[8,4,4,64,128]{4,0,3,2,1:T(8,128)(2,1)S(1)}, bf16[8,3,4,64,128]{4,0,3,2,1:T(8,128)(2,1)S(1)}) fusion(bf16[8,2,4,64,128]{4,3,2,1,0:T(8,128)(2,1)S(1)} %copy-done.4, bf16[8,4,4,64,128]{4,0,3,2,1:T(8,128)(2,1)S(1)} %get-tuple-element.252, ...), kind=kLoop, calls=%fused_computation.228 | loop fusion | bytes 4194304
  18.1 8.2 %collective-permute-done.1 = bf16[8,1,4,64,128]{4,0,3,2,1:T(8,128)(2,1)S(1)} collective-permute-done((bf16[8,1,4,64,128]{4,0,3,2,1:T(8,128)(2,1)S(1)}, bf16[8,1,4,64,128]{4,0,3,2,1:T(8,128)(2,1)S(1)}, u32[]{:S(2)}, u32[]{:S(2)}) %collective-permute-start.1) | collective-permute-done | bytes 524320 | tf_op jit(solution)/shard_map/ppermute | solution.py:15
  26.5 1.1 %copy-done.5 = bf16[8,3,4,64,128]{4,0,3,2,1:T(8,128)(2,1)} copy-done((bf16[8,3,4,64,128]{4,0,3,2,1:T(8,128)(2,1)}, bf16[8,3,4,64,128]{4,0,3,2,1:T(8,128)(2,1)S(1)}, u32[]{:S(2)}) %copy-start.5) | copy-done | bytes 1572888
  27.6 1.0 fusion.115
  28.7 1.9 %collective-permute-start.2 = (bf16[8,4,1,64,128]{4,0,3,2,1:T(8,128)(2,1)}, bf16[8,4,1,64,128]{4,0,3,2,1:T(8,128)(2,1)}, u32[]{:S(2)}, u32[]{:S(2)}) collective-permute-start(bf16[8,4,1,64,128]{4,0,3,2,1:T(8,128)(2,1)} %get-tuple-element.146), channel_id=1, source_target_pairs={{0,2},{2,4},{4,6},{1,3},{3,5},{5,7},{8,10},{10,12},{12,14},{9,11},... | collective-permute-start | bytes 1572872 | tf_op jit(solution)/shard_map/ppermute | solution.py:12
  31.1 4.0 %collective-permute-start.3 = (bf16[8,4,1,64,128]{4,0,3,2,1:T(8,128)(2,1)}, bf16[8,4,1,64,128]{4,0,3,2,1:T(8,128)(2,1)S(1)}, u32[]{:S(2)}, u32[]{:S(2)}) collective-permute-start(bf16[8,4,1,64,128]{4,0,3,2,1:T(8,128)(2,1)} %get-tuple-element.145), channel_id=1, source_target_pairs={{2,0},{4,2},{6,4},{3,1},{5,3},{7,5},{10,8},{12,10},{14,12},{11,9},... | collective-permute-start | bytes 1572872 | tf_op jit(solution)/shard_map/ppermute | solution.py:15
  35.1 1.1 %fusion.5 = bf16[8,2,4,66,130]{4,0,3,2,1:T(8,128)(2,1)S(1)} fusion(bf16[8,2,4,1,128]{4,0,3,2,1:T(8,128)(2,1)S(1)} %collective-permute-done.5, bf16[8,2,4,64,128]{4,0,3,2,1:T(8,128)(2,1)S(1)} %copy.42, bf16[8,2,4,1,128]{4,0,3,2,1:T(8,128)(2,1)S(1)} %collective-permute-done.4), kind=kLoop, calls=%fused_computation.103 | loop fusion | flops 6589440 | bytes 2179584 | tf_op jit(solution)/shard_map/concatenate | solution.py:16
  36.2 3.3 %collective-permute-done.2 = bf16[8,4,1,64,128]{4,0,3,2,1:T(8,128)(2,1)} collective-permute-done((bf16[8,4,1,64,128]{4,0,3,2,1:T(8,128)(2,1)}, bf16[8,4,1,64,128]{4,0,3,2,1:T(8,128)(2,1)}, u32[]{:S(2)}, u32[]{:S(2)}) %collective-permute-start.2) | collective-permute-done | bytes 524320 | tf_op jit(solution)/shard_map/ppermute | solution.py:12
  39.5 0.8 constant_dynamic-update-slice_fusion.150
  40.3 1.6 %collective-permute-done.3 = bf16[8,4,1,64,128]{4,0,3,2,1:T(8,128)(2,1)S(1)} collective-permute-done((bf16[8,4,1,64,128]{4,0,3,2,1:T(8,128)(2,1)}, bf16[8,4,1,64,128]{4,0,3,2,1:T(8,128)(2,1)S(1)}, u32[]{:S(2)}, u32[]{:S(2)}) %collective-permute-start.3) | collective-permute-done | bytes 524320 | tf_op jit(solution)/shard_map/ppermute | solution.py:15
  41.9 0.8 constant_dynamic-update-slice_fusion.147
  42.8 1.1 %constant_dynamic-update-slice_fusion.144 = (bf16[144,2,4,8,128]{4,0,3,2,1:T(8,128)(2,1)S(1)}, bf16[144,2,4,8,128]{4,0,3,2,1:T(8,128)(2,1)S(1)}, bf16[144,2,4,8,...) fusion(bf16[144,2,4,8,128]{4,0,3,2,1:T(8,128)(2,1)S(1)} %consta, ...), kind=kLoop, calls=%fused_computation.366 | loop fusion | flops 2097145 | bytes 3670016
  44.2 0.9 constant_dynamic-update-slice_fusion.129
  45.1 0.4 copy-done.6
  45.6 0.8 constant_dynamic-update-slice_fusion.111
  46.6 1.0 constant_dynamic-update-slice_fusion.126
  48.2 1.0 constant_dynamic-update-slice_fusion.108
  49.7 0.5 constant_dynamic-update-slice_fusion.141
  50.4 0.6 constant_dynamic-update-slice_fusion.139
  51.0 0.5 constant_dynamic-update-slice_fusion.138
  51.8 0.6 constant_dynamic-update-slice_fusion.136
  52.4 0.5 constant_dynamic-update-slice_fusion.135
  53.2 0.6 constant_dynamic-update-slice_fusion.133
  53.8 0.5 constant_dynamic-update-slice_fusion.158
  54.3 0.5 constant_dynamic-update-slice_fusion.157
  54.8 1.2 %constant_dynamic-update-slice_fusion.156 = (bf16[8,2,4,64,128]{4,0,3,2,1:T(8,128)(2,1)S(1)}, bf16[8,2,4,8,128]{4,0,3,2,1:T(8,128)(2,1)}) fusion(bf16[8,2,4,64,128]{4,0,3,2,1:T(8,128)(2,1)S(1)} %get-tuple-element.285, f32[8]{0:T(128)S(1)} %get-tuple-element.282, bf16[144,2,4,8,128]{4,0,3,2,1:T(8,128)(2,1)S(1)} %get-tuple-element.98, ...), kind=kOutput, calls=%fused_computation.378 | convolution fusion | flops 19206656 | bytes 2757120 | tf_op jit(solution)/shard_map/om,mijkl->oijkl/dot_general | solution.py:50
  56.0 1.2 %constant_dynamic-update-slice_fusion.155 = (bf16[8,2,4,64,128]{4,0,3,2,1:T(8,128)(2,1)S(1)}, bf16[8,2,4,8,128]{4,0,3,2,1:T(8,128)(2,1)}) fusion(bf16[8,2,4,64,128]{4,0,3,2,1:T(8,128)(2,1)S(1)} %get-tuple-element.287, f32[8]{0:T(128)S(1)} %get-tuple-element.282, bf16[144,2,4,8,128]{4,0,3,2,1:T(8,128)(2,1)S(1)} %get-tuple-element.97, ...), kind=kOutput, calls=%fused_computation.377 | convolution fusion | flops 19206656 | bytes 2757120 | tf_op jit(solution)/shard_map/om,mijkl->oijkl/dot_general | solution.py:50
  57.1 1.2 %constant_dynamic-update-slice_fusion.154 = (bf16[8,2,4,64,128]{4,0,3,2,1:T(8,128)(2,1)S(1)}, bf16[8,2,4,8,128]{4,0,3,2,1:T(8,128)(2,1)}) fusion(bf16[8,2,4,64,128]{4,0,3,2,1:T(8,128)(2,1)S(1)} %get-tuple-element.289, f32[8]{0:T(128)S(1)} %get-tuple-element.282, bf16[144,2,4,8,128]{4,0,3,2,1:T(8,128)(2,1)S(1)} %get-tuple-element.96, ...), kind=kOutput, calls=%fused_computation.376 | convolution fusion | flops 19206656 | bytes 2757120 | tf_op jit(solution)/shard_map/om,mijkl->oijkl/dot_general | solution.py:50
  58.3 1.2 %constant_dynamic-update-slice_fusion.153 = (bf16[8,2,4,64,128]{4,0,3,2,1:T(8,128)(2,1)S(1)}, bf16[8,2,4,8,128]{4,0,3,2,1:T(8,128)(2,1)}) fusion(bf16[8,2,4,64,128]{4,0,3,2,1:T(8,128)(2,1)S(1)} %get-tuple-element.291, f32[8]{0:T(128)S(1)} %get-tuple-element.282, bf16[144,2,4,8,128]{4,0,3,2,1:T(8,128)(2,1)S(1)} %get-tuple-element.95, ...), kind=kOutput, calls=%fused_computation.375 | convolution fusion | flops 19206656 | bytes 2757120 | tf_op jit(solution)/shard_map/om,mijkl->oijkl/dot_general | solution.py:50
  59.4 0.5 constant_dynamic-update-slice_fusion.152
  59.9 0.5 constant_dynamic-update-slice_fusion.151
  60.6 3.5 %collective-permute-start.6 = (bf16[8,1,4,64,128]{4,0,3,2,1:T(8,128)(2,1)S(1)}, bf16[8,1,4,64,128]{4,0,3,2,1:T(8,128)(2,1)S(1)}, u32[]{:S(2)}, u32[]{:S(2)}) collective-permute-start(bf16[8,1,4,64,128]{4,0,3,2,1:T(8,128)(2,1)S(1)} %get-tuple-element.210), channel_id=1, source_target_pairs={{0,8},{8,16},{16,24},{1,9},{9,17},{17,25},{2,10},{10,18},{18,26},{... | collective-permute-start | bytes 1572872 | tf_op jit(solution)/shard_map/ppermute | solution.py:12
  64.0 1.3 %collective-permute-start.7 = (bf16[8,1,4,64,128]{4,0,3,2,1:T(8,128)(2,1)S(1)}, bf16[8,1,4,64,128]{4,0,3,2,1:T(8,128)(2,1)S(1)}, u32[]{:S(2)}, u32[]{:S(2)}) collective-permute-start(bf16[8,1,4,64,128]{4,0,3,2,1:T(8,128)(2,1)S(1)} %get-tuple-element.211), channel_id=1, source_target_pairs={{8,0},{16,8},{24,16},{9,1},{17,9},{25,17},{10,2},{18,10},{26,18},{... | collective-permute-start | bytes 1572872 | tf_op jit(solution)/shard_map/ppermute | solution.py:15
  65.3 5.3 %collective-permute-done.6 = bf16[8,1,4,64,128]{4,0,3,2,1:T(8,128)(2,1)S(1)} collective-permute-done((bf16[8,1,4,64,128]{4,0,3,2,1:T(8,128)(2,1)S(1)}, bf16[8,1,4,64,128]{4,0,3,2,1:T(8,128)(2,1)S(1)}, u32[]{:S(2)}, u32[]{:S(2)}) %collective-permute-start.6) | collective-permute-done | bytes 524320 | tf_op jit(solution)/shard_map/ppermute | solution.py:12
  70.7 4.4 %collective-permute-done.7 = bf16[8,1,4,64,128]{4,0,3,2,1:T(8,128)(2,1)S(1)} collective-permute-done((bf16[8,1,4,64,128]{4,0,3,2,1:T(8,128)(2,1)S(1)}, bf16[8,1,4,64,128]{4,0,3,2,1:T(8,128)(2,1)S(1)}, u32[]{:S(2)}, u32[]{:S(2)}) %collective-permute-start.7) | collective-permute-done | bytes 524320 | tf_op jit(solution)/shard_map/ppermute | solution.py:15
  75.1 1.1 %pad_maximum_fusion.1 = (bf16[8,4,1,64,128]{4,0,3,2,1:T(8,128)(2,1)}, bf16[8,4,1,64,128]{4,0,3,2,1:T(8,128)(2,1)}) fusion(bf16[8,1,4,64,128]{4,0,3,2,1:T(8,128)(2,1)S(1)} %collective-permute-done.7, bf16[8,2,4,64,128]{4,0,3,2,1:T(8,128)(2,1)S(1)} %get-tuple-element.297, bf16[8,1,4,64,128]{4,0,3,2,1:T(8,128)(2,1)S(1)} %collective-permute-done.6), kind=kLoop, calls=%fused_computation.535 | loop fusion | flops 1048576 | bytes 3145728 | tf_op jit(solution)/shard_map/concatenate | solution.py:16
  76.2 2.3 %collective-permute-start.9 = (bf16[8,4,1,64,128]{4,0,3,2,1:T(8,128)(2,1)}, bf16[8,4,1,64,128]{4,0,3,2,1:T(8,128)(2,1)S(1)}, u32[]{:S(2)}, u32[]{:S(2)}) collective-permute-start(bf16[8,4,1,64,128]{4,0,3,2,1:T(8,128)(2,1)} %get-tuple-element.143), channel_id=1, source_target_pairs={{2,0},{4,2},{6,4},{3,1},{5,3},{7,5},{10,8},{12,10},{14,12},{11,9},... | collective-permute-start | bytes 1572872 | tf_op jit(solution)/shard_map/ppermute | solution.py:15
  78.5 2.1 %collective-permute-start.8 = (bf16[8,4,1,64,128]{4,0,3,2,1:T(8,128)(2,1)}, bf16[8,4,1,64,128]{4,0,3,2,1:T(8,128)(2,1)}, u32[]{:S(2)}, u32[]{:S(2)}) collective-permute-start(bf16[8,4,1,64,128]{4,0,3,2,1:T(8,128)(2,1)} %get-tuple-element.144), channel_id=1, source_target_pairs={{0,2},{2,4},{4,6},{1,3},{3,5},{5,7},{8,10},{10,12},{12,14},{9,11},... | collective-permute-start | bytes 1572872 | tf_op jit(solution)/shard_map/ppermute | solution.py:12
  80.6 1.3 %collective-permute-start.10 = (bf16[8,2,4,1,128]{4,0,3,2,1:T(8,128)(2,1)S(1)}, bf16[8,2,4,1,128]{4,0,3,2,1:T(8,128)(2,1)S(1)}, u32[]{:S(2)}, u32[]{:S(2)}) collective-permute-start(bf16[8,2,4,1,128]{4,0,3,2,1:T(8,128)(2,1)S(1)} %slice.1626), channel_id=1, source_target_pairs={{0,1},{2,3},{4,5},{6,7},{8,9},{10,11},{12,13},{14,15},{16,17},{18,... | collective-permute-start | bytes 49160 | tf_op jit(solution)/shard_map/ppermute | solution.py:12
  82.4 4.8 %collective-permute-start.11 = (bf16[8,2,4,1,128]{4,0,3,2,1:T(8,128)(2,1)S(1)}, bf16[8,2,4,1,128]{4,0,3,2,1:T(8,128)(2,1)S(1)}, u32[]{:S(2)}, u32[]{:S(2)}) collective-permute-start(bf16[8,2,4,1,128]{4,0,3,2,1:T(8,128)(2,1)S(1)} %slice.1627), channel_id=1, source_target_pairs={{1,0},{3,2},{5,4},{7,6},{9,8},{11,10},{13,12},{15,14},{17,16},{19,... | collective-permute-start | bytes 49160 | tf_op jit(solution)/shard_map/ppermute | solution.py:15
  87.2 2.1 %collective-permute-done.8 = bf16[8,4,1,64,128]{4,0,3,2,1:T(8,128)(2,1)} collective-permute-done((bf16[8,4,1,64,128]{4,0,3,2,1:T(8,128)(2,1)}, bf16[8,4,1,64,128]{4,0,3,2,1:T(8,128)(2,1)}, u32[]{:S(2)}, u32[]{:S(2)}) %collective-permute-start.8) | collective-permute-done | bytes 524320 | tf_op jit(solution)/shard_map/ppermute | solution.py:12
  89.3 1.7 %pad_maximum_fusion = (bf16[8,4,5,64,128]{4,0,3,2,1:T(8,128)(2,1)S(1)}, bf16[8,4,5,64,128]{4,0,3,2,1:T(8,128)(2,1)S(1)}) fusion(bf16[8,4,1,64,128]{4,0,3,2,1:T(8,128)(2,1)S(1)} %collective-permute-done.9, bf16[8,1,4,64,128]{4,0,3,2,1:T(8,128)(2,1)S(1)} %collective-permute-done.7, bf16[8,2,4,64,128]{4,0,3,2,1:T(8,128)(2,1)S(1)} %get-tuple-element.297, ...), kind=kLoop, calls=%fused_computation.98 | loop fusion | flops 7864320 | bytes 8388608 | tf_op jit(solution)/shard_map/concatenate | solution.py:16
  95.1 0.6 constant_dynamic-update-slice_fusion.295
  96.6 0.5 constant_dynamic-update-slice_fusion.277
  97.7 0.5 constant_dynamic-update-slice_fusion.259
  98.6 0.4 constant_dynamic-update-slice_fusion.241
  99.2 0.3 constant_dynamic-update-slice_fusion.223
  99.9 0.5 fusion.53
  100.3 0.5 fusion.51
  100.8 0.5 fusion.49
  101.3 0.5 fusion.47
  101.8 0.5 fusion.45
  102.3 0.5 fusion.43
  102.8 0.5 fusion.41
  103.3 0.5 fusion.39
  103.8 1.2 %copy.78 = bf16[8,2,4,64,128]{4,3,2,1,0:T(8,128)(2,1)} copy(bf16[8,2,4,64,128]{4,0,3,2,1:T(8,128)(2,1)S(1)} %fusion.39) | data formatting | bytes 2097152 | tf_op jit(solution)/shard_map/concatenate | solution.py:53
  (119 shorter events, 9.9 us)
Async XLA Ops:
  0.0 12.8 %copy-start.11 = (bf16[2,9,8,8]{1,3,2,0:T(8,128)(2,1)S(1)}, bf16[2,9,8,8]{1,3,2,0:T(8,128)(2,1)}, u32[]{:S(2)}) copy-start(bf16[2,9,8,8]{1,3,2,0:T(8,128)(2,1)} %param.5) | copy-start | bytes 6916
  0.0 13.5 %copy-start.12 = (bf16[2,9,8,8]{1,3,2,0:T(8,128)(2,1)S(1)}, bf16[2,9,8,8]{1,3,2,0:T(8,128)(2,1)}, u32[]{:S(2)}) copy-start(bf16[2,9,8,8]{1,3,2,0:T(8,128)(2,1)} %param.6) | copy-start | bytes 6916
  1.9 15.0 %copy-start.4 = (bf16[8,2,4,64,128]{4,3,2,1,0:T(8,128)(2,1)S(1)}, bf16[8,2,4,64,128]{4,3,2,1,0:T(8,128)(2,1)}, u32[]{:S(2)}) copy-start(bf16[8,2,4,64,128]{4,3,2,1,0:T(8,128)(2,1)} %param.4) | copy-start | bytes 3145732
  2.0 14.8 %collective-permute-start = (bf16[8,1,4,64,128]{4,0,3,2,1:T(8,128)(2,1)S(1)}, bf16[8,1,4,64,128]{4,0,3,2,1:T(8,128)(2,1)S(1)}, u32[]{:S(2)}, u32[]{:S(2)}) collective-permute-start(bf16[8,1,4,64,128]{4,0,3,2,1:T(8,128)(2,1)S(1)} %get-tuple-element.248), channel_id=1, source_target_pairs={{0,8},{8,16},{16,24},{1,9},{9,17},{17,25},{2,10},{10,18},{18,26},{... | collective-permute-start | bytes 1572872 | tf_op jit(solution)/shard_map/ppermute | solution.py:12
  5.7 29.4 %collective-permute-start.4 = (bf16[8,2,4,1,128]{4,0,3,2,1:T(8,128)(2,1)S(1)}, bf16[8,2,4,1,128]{4,0,3,2,1:T(8,128)(2,1)S(1)}, u32[]{:S(2)}, u32[]{:S(2)}) collective-permute-start(bf16[8,2,4,1,128]{4,0,3,2,1:T(8,128)(2,1)S(1)} %get-tuple-element.242), channel_id=1, source_target_pairs={{0,1},{2,3},{4,5},{6,7},{8,9},{10,11},{12,13},{14,15},{16,17},{18,... | collective-permute-start | bytes 49160 | tf_op jit(solution)/shard_map/ppermute | solution.py:12
  7.0 28.1 %collective-permute-start.5 = (bf16[8,2,4,1,128]{4,0,3,2,1:T(8,128)(2,1)S(1)}, bf16[8,2,4,1,128]{4,0,3,2,1:T(8,128)(2,1)S(1)}, u32[]{:S(2)}, u32[]{:S(2)}) collective-permute-start(bf16[8,2,4,1,128]{4,0,3,2,1:T(8,128)(2,1)S(1)} %get-tuple-element.243), channel_id=1, source_target_pairs={{1,0},{3,2},{5,4},{7,6},{9,8},{11,10},{13,12},{15,14},{17,16},{19,... | collective-permute-start | bytes 49160 | tf_op jit(solution)/shard_map/ppermute | solution.py:15
  11.5 14.7 %collective-permute-start.1 = (bf16[8,1,4,64,128]{4,0,3,2,1:T(8,128)(2,1)S(1)}, bf16[8,1,4,64,128]{4,0,3,2,1:T(8,128)(2,1)S(1)}, u32[]{:S(2)}, u32[]{:S(2)}) collective-permute-start(bf16[8,1,4,64,128]{4,0,3,2,1:T(8,128)(2,1)S(1)} %get-tuple-element.247), channel_id=1, source_target_pairs={{8,0},{16,8},{24,16},{9,1},{17,9},{25,17},{10,2},{18,10},{26,18},{... | collective-permute-start | bytes 1572872 | tf_op jit(solution)/shard_map/ppermute | solution.py:15
  18.0 9.6 %copy-start.7 = (bf16[8,3,4,64,128]{4,0,3,2,1:T(8,128)(2,1)}, bf16[8,3,4,64,128]{4,0,3,2,1:T(8,128)(2,1)S(1)}, u32[]{:S(2)}) copy-start(bf16[8,3,4,64,128]{4,0,3,2,1:T(8,128)(2,1)S(1)} %get-tuple-element.246) | copy-start | bytes 4718596
  18.1 12.5 %copy-start.13 = (f32[2,8]{1,0:T(2,128)S(1)}, f32[2,8]{1,0:T(2,128)}, u32[]{:S(2)}) copy-start(f32[2,8]{1,0:T(2,128)} %param.7) | copy-start | bytes 196
  26.5 1.2 %copy-start.5 = (bf16[8,3,4,64,128]{4,0,3,2,1:T(8,128)(2,1)}, bf16[8,3,4,64,128]{4,0,3,2,1:T(8,128)(2,1)S(1)}, u32[]{:S(2)}) copy-start(bf16[8,3,4,64,128]{4,0,3,2,1:T(8,128)(2,1)S(1)} %get-tuple-element.249) | copy-start | bytes 4718596
  28.7 10.8 %collective-permute-start.2 = (bf16[8,4,1,64,128]{4,0,3,2,1:T(8,128)(2,1)}, bf16[8,4,1,64,128]{4,0,3,2,1:T(8,128)(2,1)}, u32[]{:S(2)}, u32[]{:S(2)}) collective-permute-start(bf16[8,4,1,64,128]{4,0,3,2,1:T(8,128)(2,1)} %get-tuple-element.146), channel_id=1, source_target_pairs={{0,2},{2,4},{4,6},{1,3},{3,5},{5,7},{8,10},{10,12},{12,14},{9,11},... | collective-permute-start | bytes 1572872 | tf_op jit(solution)/shard_map/ppermute | solution.py:12
  31.1 9.2 %copy-start.8 = (bf16[8,3,4,64,128]{4,0,3,2,1:T(8,128)(2,1)S(1)}, bf16[8,3,4,64,128]{4,0,3,2,1:T(8,128)(2,1)}, u32[]{:S(2)}) copy-start(bf16[8,3,4,64,128]{4,0,3,2,1:T(8,128)(2,1)} %copy-done.7) | copy-start | bytes 4718596
  31.1 10.8 %collective-permute-start.3 = (bf16[8,4,1,64,128]{4,0,3,2,1:T(8,128)(2,1)}, bf16[8,4,1,64,128]{4,0,3,2,1:T(8,128)(2,1)S(1)}, u32[]{:S(2)}, u32[]{:S(2)}) collective-permute-start(bf16[8,4,1,64,128]{4,0,3,2,1:T(8,128)(2,1)} %get-tuple-element.145), channel_id=1, source_target_pairs={{2,0},{4,2},{6,4},{3,1},{5,3},{7,5},{10,8},{12,10},{14,12},{11,9},... | collective-permute-start | bytes 1572872 | tf_op jit(solution)/shard_map/ppermute | solution.py:15
  44.1 1.4 %copy-start.6 = (bf16[8,3,4,64,128]{4,0,3,2,1:T(8,128)(2,1)S(1)}, bf16[8,3,4,64,128]{4,0,3,2,1:T(8,128)(2,1)}, u32[]{:S(2)}) copy-start(bf16[8,3,4,64,128]{4,0,3,2,1:T(8,128)(2,1)} %copy-done.5) | copy-start | bytes 4718596
  60.5 21.4 %copy-start.10 = (bf16[8,9,8]{1,2,0:T(8,128)(2,1)S(1)}, bf16[8,9,8]{1,2,0:T(8,128)(2,1)}, u32[]{:S(2)}) copy-start(bf16[8,9,8]{1,2,0:T(8,128)(2,1)} %get-tuple-element.277) | copy-start | bytes 3460
  60.5 21.7 %copy-start.9 = (bf16[8,9,8]{1,2,0:T(8,128)(2,1)S(1)}, bf16[8,9,8]{1,2,0:T(8,128)(2,1)}, u32[]{:S(2)}) copy-start(bf16[8,9,8]{1,2,0:T(8,128)(2,1)} %get-tuple-element.279) | copy-start | bytes 3460
  60.6 10.1 %collective-permute-start.6 = (bf16[8,1,4,64,128]{4,0,3,2,1:T(8,128)(2,1)S(1)}, bf16[8,1,4,64,128]{4,0,3,2,1:T(8,128)(2,1)S(1)}, u32[]{:S(2)}, u32[]{:S(2)}) collective-permute-start(bf16[8,1,4,64,128]{4,0,3,2,1:T(8,128)(2,1)S(1)} %get-tuple-element.210), channel_id=1, source_target_pairs={{0,8},{8,16},{16,24},{1,9},{9,17},{17,25},{2,10},{10,18},{18,26},{... | collective-permute-start | bytes 1572872 | tf_op jit(solution)/shard_map/ppermute | solution.py:12
  64.0 11.1 %collective-permute-start.7 = (bf16[8,1,4,64,128]{4,0,3,2,1:T(8,128)(2,1)S(1)}, bf16[8,1,4,64,128]{4,0,3,2,1:T(8,128)(2,1)S(1)}, u32[]{:S(2)}, u32[]{:S(2)}) collective-permute-start(bf16[8,1,4,64,128]{4,0,3,2,1:T(8,128)(2,1)S(1)} %get-tuple-element.211), channel_id=1, source_target_pairs={{8,0},{16,8},{24,16},{9,1},{17,9},{25,17},{10,2},{18,10},{26,18},{... | collective-permute-start | bytes 1572872 | tf_op jit(solution)/shard_map/ppermute | solution.py:15
  76.2 11.0 %collective-permute-start.9 = (bf16[8,4,1,64,128]{4,0,3,2,1:T(8,128)(2,1)}, bf16[8,4,1,64,128]{4,0,3,2,1:T(8,128)(2,1)S(1)}, u32[]{:S(2)}, u32[]{:S(2)}) collective-permute-start(bf16[8,4,1,64,128]{4,0,3,2,1:T(8,128)(2,1)} %get-tuple-element.143), channel_id=1, source_target_pairs={{2,0},{4,2},{6,4},{3,1},{5,3},{7,5},{10,8},{12,10},{14,12},{11,9},... | collective-permute-start | bytes 1572872 | tf_op jit(solution)/shard_map/ppermute | solution.py:15
  78.5 10.8 %collective-permute-start.8 = (bf16[8,4,1,64,128]{4,0,3,2,1:T(8,128)(2,1)}, bf16[8,4,1,64,128]{4,0,3,2,1:T(8,128)(2,1)}, u32[]{:S(2)}, u32[]{:S(2)}) collective-permute-start(bf16[8,4,1,64,128]{4,0,3,2,1:T(8,128)(2,1)} %get-tuple-element.144), channel_id=1, source_target_pairs={{0,2},{2,4},{4,6},{1,3},{3,5},{5,7},{8,10},{10,12},{12,14},{9,11},... | collective-permute-start | bytes 1572872 | tf_op jit(solution)/shard_map/ppermute | solution.py:12
  80.6 6.6 %collective-permute-start.10 = (bf16[8,2,4,1,128]{4,0,3,2,1:T(8,128)(2,1)S(1)}, bf16[8,2,4,1,128]{4,0,3,2,1:T(8,128)(2,1)S(1)}, u32[]{:S(2)}, u32[]{:S(2)}) collective-permute-start(bf16[8,2,4,1,128]{4,0,3,2,1:T(8,128)(2,1)S(1)} %slice.1626), channel_id=1, source_target_pairs={{0,1},{2,3},{4,5},{6,7},{8,9},{10,11},{12,13},{14,15},{16,17},{18,... | collective-permute-start | bytes 49160 | tf_op jit(solution)/shard_map/ppermute | solution.py:12
  82.4 11.8 %collective-permute-start.11 = (bf16[8,2,4,1,128]{4,0,3,2,1:T(8,128)(2,1)S(1)}, bf16[8,2,4,1,128]{4,0,3,2,1:T(8,128)(2,1)S(1)}, u32[]{:S(2)}, u32[]{:S(2)}) collective-permute-start(bf16[8,2,4,1,128]{4,0,3,2,1:T(8,128)(2,1)S(1)} %slice.1627), channel_id=1, source_target_pairs={{1,0},{3,2},{5,4},{7,6},{9,8},{11,10},{13,12},{15,14},{17,16},{19,... | collective-permute-start | bytes 49160 | tf_op jit(solution)/shard_map/ppermute | solution.py:15
  91.5 0.9 copy-start.3
  91.5 1.0 copy-start
  91.8 0.9 copy-start.1
  91.8 1.0 copy-start.2
where the time goes:
time: 106 us; the launch traced here: 105 us
  starting transfers between devices  31.8 us (30%)
  waiting for transfers between devices  27.7 us (26%)
  local copies, waits for them, and re-layouts  21.1 us (20%)
  other arithmetic  12.9 us (12%)
  matrix products  10.6 us (10%)
  between operations  1.07 us (1%)
    ppermute x6, starting transfers between devices, padded(): lax.ppermute(lax.slice_in_dim(block, 0, width, axis=dim), axis, backward)  18.1 us
    ppermute x6, waiting for transfers between devices, padded(): lax.ppermute(lax.slice_in_dim(block, 0, width, axis=dim), axis, backward)  14.2 us
    ppermute x6, starting transfers between devices, padded(): lax.ppermute(lax.slice_in_dim(block, block.shape[dim] - width, None, axis...  13.7 us
    ppermute x6, waiting for transfers between devices, padded(): lax.ppermute(lax.slice_in_dim(block, block.shape[dim] - width, None, axis...  13.5 us
    unnamed x82, local copies, waits for them, and re-layouts  13.1 us
    dot_general x16, matrix products, apply_layer(): jnp.einsum('om,mijkl->oijkl', kernel, stacked, preferred_element_type=jnp...  10.6 us
    unnamed x31, other arithmetic  8.99 us
    concatenate x3, other arithmetic, padded(): block = jnp.concatenate([low, block, high], axis=dim)  3.9 us
  transfers between devices with their start and end apart: 12, of which 7 were waited for; matrix products, arithmetic and copies ran while one was open for 10% of the time, Pallas kernels for 0%

commit v1 on v0

v1 whole, which is shorter than its diff:
```python
import functools

import jax
import jax.numpy as jnp
from jax import lax
from jax.experimental import pallas as pl
from jax.experimental.pallas import tpu as pltpu
from jax.sharding import PartitionSpec as P

BAND = 32
EDGE = 16
VMEM_LIMIT = 56 * 1024 * 1024
F32 = jnp.float32
BF16 = jnp.bfloat16


def in_vmem(count):
    return [pl.BlockSpec(memory_space=pltpu.VMEM)] * count


def call(body, outs, scratch=(), flops=0, moved=0):
    def run(*args):
        return pl.pallas_call(
            body,
            out_shape=outs,
            in_specs=in_vmem(len(args)),
            out_specs=tuple(in_vmem(len(outs))),
            scratch_shapes=list(scratch),
            compiler_params=pltpu.CompilerParams(vmem_limit_bytes=VMEM_LIMIT),
            cost_estimate=pl.CostEstimate(flops=flops, bytes_accessed=moved, transcendentals=0),
        )(*args)

    return run


def dot(a, b):
    return jnp.dot(a, b, preferred_element_type=F32)


def build_body(taps, channels, table_ref, src_ref, tgt_ref, low_ref, high_ref):
    span = channels * BAND
    small = channels * EDGE
    row = lax.broadcasted_iota(jnp.int32, (span, span), 0)
    col = lax.broadcasted_iota(jnp.int32, (span, span), 1)
    shift = (row % BAND) - (col % BAND)
    row_s = lax.broadcasted_iota(jnp.int32, (span, small), 0) % BAND
    col_s = lax.broadcasted_iota(jnp.int32, (span, small), 1) % EDGE
    at_low = (row_s == 0) & (col_s == EDGE - 1)
    at_high = (row_s == BAND - 1) & (col_s == 0)
    pick_r = lax.broadcasted_iota(jnp.int32, (span, channels), 0) // BAND
    pick_c = lax.broadcasted_iota(jnp.int32, (span, channels), 1)
    spread = (pick_r == pick_c).astype(BF16)
    layers = table_ref.shape[0]
    width = taps * channels
    gate_r = lax.broadcasted_iota(jnp.int32, (width, span), 0)
    gate_c = lax.broadcasted_iota(jnp.int32, (width, span), 1) // BAND
    gate_rs = lax.broadcasted_iota(jnp.int32, (width, small), 0)
    gate_cs = lax.broadcasted_iota(jnp.int32, (width, small), 1) // EDGE
    for layer in range(layers):
        tall = dot(spread, table_ref[layer]).astype(BF16)

        def full(tap):
            return dot(tall, (gate_r == gate_c + tap * channels).astype(BF16))

        def part(tap):
            return dot(tall, (gate_rs == gate_cs + tap * channels).astype(BF16))

        for tap in range(9):
            first, second = divmod(tap, 3)
            src_ref[layer, first, :, second * span : (second + 1) * span] = jnp.where(
                shift == 0, full(tap), 0.0
            ).astype(BF16)
        for second in range(3):
            band = jnp.where(shift == 1, full(9 + second), 0.0)
            band = jnp.where(shift == 0, full(12 + second), band)
            band = jnp.where(shift == -1, full(15 + second), band)
            tgt_ref[layer, :, second * span : (second + 1) * span] = band.astype(BF16)
            cut = slice(second * small, (second + 1) * small)
            low_ref[layer, :, cut] = jnp.where(at_low, part(9 + second), 0.0).astype(BF16)
            high_ref[layer, :, cut] = jnp.where(at_high, part(15 + second), 0.0).astype(BF16)


def build(src_weight, tgt_weight):
    layers, _, outs, ins = src_weight.shape
    both = jnp.concatenate([src_weight, tgt_weight], axis=1)
    taps = both.shape[1]
    table = jnp.transpose(both, (0, 2, 1, 3)).reshape(layers, outs, taps * ins)
    span, small = ins * BAND, ins * EDGE
    shape = jax.ShapeDtypeStruct
    return call(
        functools.partial(build_body, taps, ins),
        (
            shape((layers, 3, span, 3 * span), BF16),
            shape((layers, span, 3 * span), BF16),
            shape((layers, span, 3 * small), BF16),
            shape((layers, span, 3 * small), BF16),
        ),
        flops=2 * layers * taps * span * span * taps * ins,
        moved=layers * 14 * span * span * 2,
    )(table)


def source_rows(x_ref, left_ref, right_ref, i, start, size):
    cols = x_ref.shape[2]
    channels = x_ref.shape[0]
    tiles = [left_ref[:, i, start : start + size, :]]
    tiles += [x_ref[:, i, j, start : start + size, :] for j in range(cols)]
    tiles += [right_ref[:, i, start : start + size, :]]
    return [t.reshape(channels * size, t.shape[-1]) for t in tiles]


def src_operand(tiles, cols):
    return jnp.concatenate([jnp.concatenate(tiles[b : b + cols], axis=1) for b in range(3)], axis=0)


def edge_body(layer, x_ref, left_ref, right_ref, src_ref, down_ref, up_ref):
    channels, rows, cols, depth, width = x_ref.shape
    for start in range(0, depth, BAND):
        for i, first, out_ref in ((rows - 1, 0, down_ref), (0, 2, up_ref)):
            tiles = source_rows(x_ref, left_ref, right_ref, i, start, BAND)
            got = dot(src_ref[layer, first], src_operand(tiles, cols)).astype(BF16)
            for j in range(cols):
                out_ref[:, j, start : start + BAND, :] = got[:, j * width : (j + 1) * width].reshape(
                    channels, BAND, width
                )


def shifted(tile, step):
    lane = lax.broadcasted_iota(jnp.int32, tile.shape, 1)
    width = tile.shape[1]
    rolled = pltpu.roll(tile.astype(F32), step % width, 1)
    gone = 0 if step == 1 else width - 1
    return jnp.where(lane == gone, 0.0, rolled).astype(BF16)


def main_body(
    layer, x_ref, left_ref, right_ref, lowy_ref, highy_ref, src_ref, tgt_ref, lo_ref, hi_ref, bias_ref, acc_ref, side_ref
):
    channels, rows, cols, depth, width = x_ref.shape
    span = channels * BAND
    bands = depth // BAND
    out_channel = lax.broadcasted_iota(jnp.int32, (span, 1), 0) // BAND
    bias = jnp.zeros((span, 1), F32)
    for o in range(channels):
        bias = jnp.where(out_channel == o, bias_ref[layer, o], bias)

    def three(read, size):
        lanes = []
        for step in (1, 0, -1):
            tiles = [read(j).reshape(channels * size, width) for j in range(cols)]
            if step:
                tiles = [shifted(t, step) for t in tiles]
            lanes.append(jnp.concatenate(tiles, axis=1))
        return lanes

    for i in range(rows):
        for q in range(bands):
            for n, value in enumerate(three(lambda j: x_ref[:, i, j, q * BAND : (q + 1) * BAND, :], BAND)):
                side_ref[q, n] = value
        low_y = jnp.concatenate(three(lambda j: lowy_ref[:, i, j], EDGE), axis=0)
        high_y = jnp.concatenate(three(lambda j: highy_ref[:, i, j], EDGE), axis=0)
        for q in range(bands):
            total = jnp.broadcast_to(bias, (span, cols * width))
            for a in range(3):
                if 0 <= i + a - 1 < rows:
                    tiles = source_rows(x_ref, left_ref, right_ref, i + a - 1, q * BAND, BAND)
                    total = total + dot(src_ref[layer, a], src_operand(tiles, cols))
            total = total + dot(tgt_ref[layer], side_ref[q].reshape(3 * span, cols * width))

            def near(band, start):
                parts = [
                    side_ref[band, n].reshape(channels, BAND, cols * width)[:, start : start + EDGE].reshape(
                        channels * EDGE, cols * width
                    )
                    for n in range(3)
                ]
                return jnp.concatenate(parts, axis=0)

            total = total + dot(lo_ref[layer], low_y if q == 0 else near(q - 1, BAND - EDGE))
            total = total + dot(hi_ref[layer], high_y if q == bands - 1 else near(q + 1, 0))
            for j in range(cols):
                acc_ref[:, i, j, q * BAND : (q + 1) * BAND, :] = total[:, j * width : (j + 1) * width].reshape(
                    channels, BAND, width
                )


def finish_body(last, x_ref, acc_ref, fromlow_ref, fromhigh_ref, out_ref, *more):
    channels, rows, cols, depth, width = x_ref.shape
    for i in range(rows):
        for j in range(cols):
            total = acc_ref[:, i, j]
            if i == 0:
                total = total + fromlow_ref[:, j].astype(F32)
            if i == rows - 1:
                total = total + fromhigh_ref[:, j].astype(F32)
            value = (x_ref[:, i, j].astype(F32) + jnp.maximum(total, 0.0)).astype(BF16)
            out_ref[:, i, j] = value
            if not last:
                first_ref, final_ref, top_ref, bottom_ref = more
                if j == 0:
                    first_ref[:, i] = value
                if j == cols - 1:
                    final_ref[:, i] = value
                top_ref[:, i, j] = value[:, :EDGE]
                bottom_ref[:, i, j] = value[:, depth - EDGE :]


def beside(block_up, block_down, axis):
    count = lax.axis_size(axis)
    forward = [(i, i + 1) for i in range(count - 1)]
    backward = [(i + 1, i) for i in range(count - 1)]
    return lax.ppermute(block_up, axis, forward), lax.ppermute(block_down, axis, backward)


def target_halo(top, bottom):
    axis = "trow"
    count = lax.axis_size(axis)
    if count != 2:
        return beside(bottom, top, axis)
    me = lax.axis_index(axis)
    both = lax.all_gather(jnp.where(me == 0, bottom, top), axis)
    zero = jnp.zeros_like(top)
    return jnp.where(me == 0, zero, both[0]), jnp.where(me == 0, both[1], zero)


def shards(volume, src_weight, tgt_weight, bias):
    layers = src_weight.shape[0]
    channels, rows, cols, depth, width = volume.shape
    shape = jax.ShapeDtypeStruct
    state = volume
    edges = (volume[:, :, 0], volume[:, :, cols - 1], volume[:, :, :, :EDGE], volume[:, :, :, depth - EDGE :])
    src, tgt, low, high = build(src_weight, tgt_weight)
    size = channels * rows * cols * depth * width
    for layer in range(layers):
        first, final, top, bottom = edges
        left, right = beside(final, first, "scol")
        low_y, high_y = target_halo(top, bottom)
        row = shape((channels, cols, depth, width), BF16)
        down, up = call(
            functools.partial(edge_body, layer), (row, row), flops=2 * size // rows * 2 * 3 * channels * BAND, moved=size * 2
        )(state, left, right, src)
        from_low, from_high = beside(down, up, "srow")
        (acc,) = call(
            functools.partial(main_body, layer),
            (shape(volume.shape, F32),),
            scratch=[pltpu.VMEM((depth // BAND, 3, channels * BAND, cols * width), BF16)],
            flops=2 * size * 12 * channels * BAND,
            moved=size * 8,
        )(state, left, right, low_y, high_y, src, tgt, low, high, bias)
        last = layer == layers - 1
        outs = (shape(volume.shape, BF16),)
        if not last:
            outs += tuple(shape(e.shape, BF16) for e in edges)
        state, *edges = call(functools.partial(finish_body, last), outs, flops=size, moved=size * 10)(
            state, acc, from_low, from_high
        )
    return state


def solution(mesh):
    return jax.shard_map(
        shards,
        mesh=mesh,
        in_specs=(P(None, "srow", "scol", "trow", None), P(), P(), P()),
        out_specs=P(None, "srow", "scol", "trow", None),
        check_vma=False,
    )
```

time: 106 us -> 94.4 us (0.89)
  the two profiles are of different devices: /device:TPU:6 before, /device:TPU:0 now
where the time goes in v1:
time: 94.4 us; the launch traced here: 93.9 us
  Pallas kernels  34.9 us (37%)
  blocking collectives  19.9 us (21%)
  starting transfers between devices  17.4 us (18%)
  waiting for transfers between devices  11.7 us (12%)
  local copies, waits for them, and re-layouts  5.15 us (5%)
  other arithmetic  4.67 us (5%)
    pallas_call x7, Pallas kernels, run(): pl.pallas_call(body, out_shape=outs, in_specs=in_vmem(len(args)), out_spe...  34.9 us
    all_gather x2, blocking collectives, target_halo(): both = lax.all_gather(jnp.where(me == 0, bottom, top), axis)  19.9 us
    ppermute x4, starting transfers between devices, beside(): lax.ppermute(block_up, axis, forward)  12.3 us
    ppermute x4, waiting for transfers between devices, beside(): lax.ppermute(block_down, axis, backward)  8.08 us
    ppermute x4, starting transfers between devices, beside(): lax.ppermute(block_down, axis, backward)  5.17 us
    ppermute x4, waiting for transfers between devices, beside(): lax.ppermute(block_up, axis, forward)  3.66 us
    unnamed x16, local copies, waits for them, and re-layouts  3.19 us
    select_n x2, other arithmetic, target_halo(): both = lax.all_gather(jnp.where(me == 0, bottom, top), axis)  2.07 us
  transfers between devices with their start and end apart: 8, of which 4 were waited for; matrix products, arithmetic and copies ran while one was open for 6% of the time, Pallas kernels for 21%

profile of v1, /device:TPU:0, one launch (start us, length us, event | category | flops | bytes accessed | tf_op | source)
XLA Modules:
  0.0 93.9 jit_solution(31112482902695688)
XLA Ops:
  0.0 1.1 %slice_bitcast_fusion = (bf16[8,2,64,128]{3,2,1,0:T(8,128)(2,1)S(1)}, bf16[8,2,64,128]{3,2,1,0:T(8,128)(2,1)S(1)}) fusion(bf16[8,2,4,64,128]{4,3,2,1,0:T(8,128)(2,1)} %x_ref.5), kind=kLoop, calls=%fused_computation.5 | loop fusion | bytes 1048576 | tf_op jit(solution)/shard_map/squeeze | solution.py:231
  1.1 1.3 %collective-permute-start.1 = (bf16[8,2,64,128]{3,2,1,0:T(8,128)(2,1)S(1)}, bf16[8,2,64,128]{3,2,1,0:T(8,128)(2,1)S(1)}, u32[]{:S(2)}, u32[]{:S(2)}) collective-permute-start(bf16[8,2,64,128]{3,2,1,0:T(8,128)(2,1)S(1)} %get-tuple-element.31), channel_id=1, source_target_pairs={{2,0},{4,2},{6,4},{3,1},{5,3},{7,5},{10,8},{12,10},{14,12},{11,9},... | collective-permute-start | bytes 786440 | tf_op jit(solution)/shard_map/ppermute | solution.py:212
  2.4 3.0 %collective-permute-start = (bf16[8,2,64,128]{3,2,1,0:T(8,128)(2,1)S(1)}, bf16[8,2,64,128]{3,2,1,0:T(8,128)(2,1)S(1)}, u32[]{:S(2)}, u32[]{:S(2)}) collective-permute-start(bf16[8,2,64,128]{3,2,1,0:T(8,128)(2,1)S(1)} %get-tuple-element.32), channel_id=1, source_target_pairs={{0,2},{2,4},{4,6},{1,3},{3,5},{5,7},{8,10},{10,12},{12,14},{9,11},... | collective-permute-start | bytes 786440 | tf_op jit(solution)/shard_map/ppermute | solution.py:212
  5.4 1.1 %slice_select_fusion.4 = bf16[8,2,4,16,128]{4,3,2,1,0:T(8,128)(2,1)S(1)} fusion(bf16[8,2,4,64,128]{4,3,2,1,0:T(8,128)(2,1)} %x_ref.5, pred[]{:T(512)S(6)} %eq.2), kind=kLoop, calls=%fused_computation.4 | loop fusion | flops 131072 | bytes 786433 | tf_op jit(solution)/shard_map/jit(_where)/select_n | solution.py:221
  6.5 0.9 maximum_bitcast_fusion
  7.4 0.2 copy.13
  7.6 0.7 reshape.15.table_ref
  8.3 4.3 %shard_map.46 = (bf16[2,3,256,768]{3,2,1,0:T(8,128)(2,1)}, bf16[2,256,768]{2,1,0:T(8,128)(2,1)}, bf16[2,256,384]{2,1,0:T(8,128)(2,1)}, bf16[2,256,384]{2,1,0:T(8,128)(2,1)}) custom-call(bf16[2,8,144]{2,1,0:T(8,128)(2,1)} %reshape.15.table_ref), custom_call_target="tpu_custom_call" | custom-call | flops 679477248 | bytes 3670016 | tf_op jit(solution)/shard_map/pallas_call | solution.py:23
  12.6 10.2 %all-gather = bf16[16,2,4,16,128]{4,3,2,1,0:T(8,128)(2,1)S(1)} all-gather(bf16[8,2,4,16,128]{4,3,2,1,0:T(8,128)(2,1)S(1)} %slice_select_fusion.4), channel_id=2, replica_groups=mesh['srow'=4,'scol'=4,'trow'=2] {'trow'}, dimensions={0}, use_global_device_ids=true | all-gather | bytes 786432 | tf_op jit(solution)/shard_map/all_gather | solution.py:221
  22.8 0.0 collective-permute-done.1.right_ref
  22.8 0.0 copy-start.4
  22.8 0.0 collective-permute-done.left_ref
  22.8 0.0 copy-start.5
  22.8 0.7 copy-done.4
  23.5 0.1 copy-done.5
  23.6 4.0 %shard_map.48 = (bf16[8,4,64,128]{3,2,1,0:T(8,128)(2,1)}, bf16[8,4,64,128]{3,2,1,0:T(8,128)(2,1)}) custom-call(bf16[8,2,4,64,128]{4,3,2,1,0:T(8,128)(2,1)} %x_ref.5, bf16[8,2,64,128]{3,2,1,0:T(8,128)(2,1)} %copy-done.5, bf16[8,2,64,128]{3,2,1,0:T(8,128)(2,1)} %copy-done.4, bf16[2,3,256,768]{3,2,1,0:T(8,128)(2,1)} %get-tuple-element.18.src_ref), custom_call_target="tpu_custom_call" | custom-call | flops 805306368 | bytes 1048576 | tf_op jit(solution)/shard_map/pallas_call | solution.py:23
  27.5 4.5 %collective-permute-start.2 = (bf16[8,4,64,128]{3,2,1,0:T(8,128)(2,1)}, bf16[8,4,64,128]{3,2,1,0:T(8,128)(2,1)S(1)}, u32[]{:S(2)}, u32[]{:S(2)}) collective-permute-start(bf16[8,4,64,128]{3,2,1,0:T(8,128)(2,1)} %get-tuple-element.22), channel_id=1, source_target_pairs={{0,8},{8,16},{16,24},{1,9},{9,17},{17,25},{2,10},{10,18},{18,26},{... | collective-permute-start | bytes 1572872 | tf_op jit(solution)/shard_map/ppermute | solution.py:212
  32.0 1.3 %collective-permute-start.3 = (bf16[8,4,64,128]{3,2,1,0:T(8,128)(2,1)}, bf16[8,4,64,128]{3,2,1,0:T(8,128)(2,1)S(1)}, u32[]{:S(2)}, u32[]{:S(2)}) collective-permute-start(bf16[8,4,64,128]{3,2,1,0:T(8,128)(2,1)} %get-tuple-element.23), channel_id=1, source_target_pairs={{8,0},{16,8},{24,16},{9,1},{17,9},{25,17},{10,2},{18,10},{26,18},{... | collective-permute-start | bytes 1572872 | tf_op jit(solution)/shard_map/ppermute | solution.py:212
  33.3 0.9 slice_select_fusion.2
  34.2 7.7 %shard_map.47.acc_ref = f32[8,2,4,64,128]{4,3,2,1,0:T(8,128)} custom-call(bf16[8,2,4,64,128]{4,3,2,1,0:T(8,128)(2,1)} %x_ref.5, bf16[8,2,64,128]{3,2,1,0:T(8,128)(2,1)} %copy-done.5, bf16[8,2,64,128]{3,2,1,0:T(8,128)(2,1)} %copy-done.4, bf16[8,2,4,16,128]{4,3,2,1,0:T(8,128)(2,1)} %get-tuple-element.36.lowy_ref, ...), custom_call_target="tpu_custom_call" | custom-call | flops 3221225472 | bytes 4194304 | tf_op jit(solution)/shard_map/pallas_call | solution.py:23
  41.9 1.8 %collective-permute-done.2.fromlow_ref = bf16[8,4,64,128]{3,2,1,0:T(8,128)(2,1)S(1)} collective-permute-done((bf16[8,4,64,128]{3,2,1,0:T(8,128)(2,1)}, bf16[8,4,64,128]{3,2,1,0:T(8,128)(2,1)S(1)}, u32[]{:S(2)}, u32[]{:S(2)}) %collective-permute-start.2) | collective-permute-done | bytes 524320 | tf_op jit(solution)/shard_map/ppermute | solution.py:212
  43.7 0.0 copy-start.2
  43.8 4.0 %collective-permute-done.3.fromhigh_ref = bf16[8,4,64,128]{3,2,1,0:T(8,128)(2,1)S(1)} collective-permute-done((bf16[8,4,64,128]{3,2,1,0:T(8,128)(2,1)}, bf16[8,4,64,128]{3,2,1,0:T(8,128)(2,1)S(1)}, u32[]{:S(2)}, u32[]{:S(2)}) %collective-permute-start.3) | collective-permute-done | bytes 524320 | tf_op jit(solution)/shard_map/ppermute | solution.py:212
  47.8 0.0 copy-done.2
  47.8 0.0 copy-start.3
  47.8 0.8 copy-done.3
  48.6 3.7 %shard_map.49 = (bf16[8,2,4,64,128]{4,3,2,1,0:T(8,128)(2,1)}, bf16[8,2,64,128]{3,2,1,0:T(8,128)(2,1)}, bf16[8,2,64,128]{3,2,1,0:T(8,128)(2,1)}, bf16[8,2,4,16,12...) custom-call(bf16[8,2,4,64,128]{4,3,2,1,0:T(8,128)(2,1)} %x_ref.5, f32[8,2,4,64,128]{4,3,2,1,0:T(8,128)} %shard_map.47.acc_ref, ...), custom_call_target="tpu_custom_call" | custom-call | flops 524288 | bytes 5242880 | tf_op jit(solution)/shard_map/pallas_call | solution.py:23
  52.3 1.3 %collective-permute-start.4 = (bf16[8,2,64,128]{3,2,1,0:T(8,128)(2,1)}, bf16[8,2,64,128]{3,2,1,0:T(8,128)(2,1)S(1)}, u32[]{:S(2)}, u32[]{:S(2)}) collective-permute-start(bf16[8,2,64,128]{3,2,1,0:T(8,128)(2,1)} %get-tuple-element.25), channel_id=1, source_target_pairs={{0,2},{2,4},{4,6},{1,3},{3,5},{5,7},{8,10},{10,12},{12,14},{9,11},... | collective-permute-start | bytes 786440 | tf_op jit(solution)/shard_map/ppermute | solution.py:212
  53.6 1.3 %collective-permute-start.5 = (bf16[8,2,64,128]{3,2,1,0:T(8,128)(2,1)}, bf16[8,2,64,128]{3,2,1,0:T(8,128)(2,1)S(1)}, u32[]{:S(2)}, u32[]{:S(2)}) collective-permute-start(bf16[8,2,64,128]{3,2,1,0:T(8,128)(2,1)} %get-tuple-element.26), channel_id=1, source_target_pairs={{2,0},{4,2},{6,4},{3,1},{5,3},{7,5},{10,8},{12,10},{14,12},{11,9},... | collective-permute-start | bytes 786440 | tf_op jit(solution)/shard_map/ppermute | solution.py:212
  54.9 1.0 %broadcast_select_fusion = bf16[8,2,4,16,128]{4,3,2,1,0:T(8,128)(2,1)S(1)} fusion(bf16[8,2,4,16,128]{4,3,2,1,0:T(8,128)(2,1)} %get-tuple-element.27, bf16[8,2,4,16,128]{4,3,2,1,0:T(8,128)(2,1)} %get-tuple-element.28, pred[]{:T(512)S(6)} %eq.2), kind=kLoop, calls=%fused_computation.7 | loop fusion | flops 131072 | bytes 786433 | tf_op jit(solution)/shard_map/jit(_where)/select_n | solution.py:221
  55.9 9.7 %all-gather.1 = bf16[16,2,4,16,128]{4,3,2,1,0:T(8,128)(2,1)S(1)} all-gather(bf16[8,2,4,16,128]{4,3,2,1,0:T(8,128)(2,1)S(1)} %broadcast_select_fusion), channel_id=3, replica_groups=mesh['srow'=4,'scol'=4,'trow'=2] {'trow'}, dimensions={0}, use_global_device_ids=true | all-gather | bytes 786432 | tf_op jit(solution)/shard_map/all_gather | solution.py:221
  65.6 0.0 collective-permute-done.4.left_ref
  65.6 0.0 copy-start.6
  65.6 0.0 collective-permute-done.5.right_ref
  65.6 0.0 copy-start.7
  65.6 0.7 copy-done.6
  66.3 0.1 copy-done.7
  66.4 3.9 %shard_map.51 = (bf16[8,4,64,128]{3,2,1,0:T(8,128)(2,1)}, bf16[8,4,64,128]{3,2,1,0:T(8,128)(2,1)}) custom-call(bf16[8,2,4,64,128]{4,3,2,1,0:T(8,128)(2,1)} %get-tuple-element.24.x_ref, bf16[8,2,64,128]{3,2,1,0:T(8,128)(2,1)} %copy-done.6, bf16[8,2,64,128]{3,2,1,0:T(8,128)(2,1)} %copy-done.7, bf16[2,3,256,768]{3,2,1,0:T(8,128)(2,1)} %get-tuple-element.18.src_ref), custom_call_target="tpu_custom_call" | custom-call | flops 805306368 | bytes 1048576 | tf_op jit(solution)/shard_map/pallas_call | solution.py:23
  70.4 3.5 %collective-permute-start.6 = (bf16[8,4,64,128]{3,2,1,0:T(8,128)(2,1)}, bf16[8,4,64,128]{3,2,1,0:T(8,128)(2,1)S(1)}, u32[]{:S(2)}, u32[]{:S(2)}) collective-permute-start(bf16[8,4,64,128]{3,2,1,0:T(8,128)(2,1)} %get-tuple-element.29), channel_id=1, source_target_pairs={{0,8},{8,16},{16,24},{1,9},{9,17},{17,25},{2,10},{10,18},{18,26},{... | collective-permute-start | bytes 1572872 | tf_op jit(solution)/shard_map/ppermute | solution.py:212
  73.8 1.3 %collective-permute-start.7 = (bf16[8,4,64,128]{3,2,1,0:T(8,128)(2,1)}, bf16[8,4,64,128]{3,2,1,0:T(8,128)(2,1)S(1)}, u32[]{:S(2)}, u32[]{:S(2)}) collective-permute-start(bf16[8,4,64,128]{3,2,1,0:T(8,128)(2,1)} %get-tuple-element.30), channel_id=1, source_target_pairs={{8,0},{16,8},{24,16},{9,1},{17,9},{25,17},{10,2},{18,10},{26,18},{... | collective-permute-start | bytes 1572872 | tf_op jit(solution)/shard_map/ppermute | solution.py:212
  75.1 0.9 slice_select_fusion
  76.0 7.7 %shard_map.50.acc_ref = f32[8,2,4,64,128]{4,3,2,1,0:T(8,128)} custom-call(bf16[8,2,4,64,128]{4,3,2,1,0:T(8,128)(2,1)} %get-tuple-element.24.x_ref, bf16[8,2,64,128]{3,2,1,0:T(8,128)(2,1)} %copy-done.6, bf16[8,2,64,128]{3,2,1,0:T(8,128)(2,1)} %copy-done.7, bf16[8,2,4,16,128]{4,3,2,1,0:T(8,128)(2,1)} %get-tuple-element.34.lowy_ref, ...), custom_call_target="tpu_custom_call" | custom-call | flops 3221225472 | bytes 4194304 | tf_op jit(solution)/shard_map/pallas_call | solution.py:23
  83.7 1.8 %collective-permute-done.6.fromlow_ref = bf16[8,4,64,128]{3,2,1,0:T(8,128)(2,1)S(1)} collective-permute-done((bf16[8,4,64,128]{3,2,1,0:T(8,128)(2,1)}, bf16[8,4,64,128]{3,2,1,0:T(8,128)(2,1)S(1)}, u32[]{:S(2)}, u32[]{:S(2)}) %collective-permute-start.6) | collective-permute-done | bytes 524320 | tf_op jit(solution)/shard_map/ppermute | solution.py:212
  85.6 0.0 copy-start
  85.6 4.0 %collective-permute-done.7.fromhigh_ref = bf16[8,4,64,128]{3,2,1,0:T(8,128)(2,1)S(1)} collective-permute-done((bf16[8,4,64,128]{3,2,1,0:T(8,128)(2,1)}, bf16[8,4,64,128]{3,2,1,0:T(8,128)(2,1)S(1)}, u32[]{:S(2)}, u32[]{:S(2)}) %collective-permute-start.7) | collective-permute-done | bytes 524320 | tf_op jit(solution)/shard_map/ppermute | solution.py:212
  89.6 0.0 copy-done
  89.6 0.0 copy-start.1
  89.6 0.8 copy-done.1
  90.4 3.5 %shard_map.52 = bf16[8,2,4,64,128]{4,3,2,1,0:T(8,128)(2,1)} custom-call(bf16[8,2,4,64,128]{4,3,2,1,0:T(8,128)(2,1)} %get-tuple-element.24.x_ref, f32[8,2,4,64,128]{4,3,2,1,0:T(8,128)} %shard_map.50.acc_ref, bf16[8,4,64,128]{3,2,1,0:T(8,128)(2,1)} %copy-done, bf16[8,4,64,128]{3,2,1,0:T(8,128)(2,1)} %copy-done.1), custom_call_target="tpu_custom_call" | custom-call | flops 524288 | bytes 5242880 | tf_op jit(solution)/shard_map/pallas_call | solution.py:23
Async XLA Ops:
  1.1 21.7 %collective-permute-start.1 = (bf16[8,2,64,128]{3,2,1,0:T(8,128)(2,1)S(1)}, bf16[8,2,64,128]{3,2,1,0:T(8,128)(2,1)S(1)}, u32[]{:S(2)}, u32[]{:S(2)}) collective-permute-start(bf16[8,2,64,128]{3,2,1,0:T(8,128)(2,1)S(1)} %get-tuple-element.31), channel_id=1, source_target_pairs={{2,0},{4,2},{6,4},{3,1},{5,3},{7,5},{10,8},{12,10},{14,12},{11,9},... | collective-permute-start | bytes 786440 | tf_op jit(solution)/shard_map/ppermute | solution.py:212
  2.4 20.4 %collective-permute-start = (bf16[8,2,64,128]{3,2,1,0:T(8,128)(2,1)S(1)}, bf16[8,2,64,128]{3,2,1,0:T(8,128)(2,1)S(1)}, u32[]{:S(2)}, u32[]{:S(2)}) collective-permute-start(bf16[8,2,64,128]{3,2,1,0:T(8,128)(2,1)S(1)} %get-tuple-element.32), channel_id=1, source_target_pairs={{0,2},{2,4},{4,6},{1,3},{3,5},{5,7},{8,10},{10,12},{12,14},{9,11},... | collective-permute-start | bytes 786440 | tf_op jit(solution)/shard_map/ppermute | solution.py:212
  22.8 0.7 copy-start.4
  22.8 0.8 copy-start.5
  27.5 16.2 %collective-permute-start.2 = (bf16[8,4,64,128]{3,2,1,0:T(8,128)(2,1)}, bf16[8,4,64,128]{3,2,1,0:T(8,128)(2,1)S(1)}, u32[]{:S(2)}, u32[]{:S(2)}) collective-permute-start(bf16[8,4,64,128]{3,2,1,0:T(8,128)(2,1)} %get-tuple-element.22), channel_id=1, source_target_pairs={{0,8},{8,16},{16,24},{1,9},{9,17},{17,25},{2,10},{10,18},{18,26},{... | collective-permute-start | bytes 1572872 | tf_op jit(solution)/shard_map/ppermute | solution.py:212
  32.0 15.8 %collective-permute-start.3 = (bf16[8,4,64,128]{3,2,1,0:T(8,128)(2,1)}, bf16[8,4,64,128]{3,2,1,0:T(8,128)(2,1)S(1)}, u32[]{:S(2)}, u32[]{:S(2)}) collective-permute-start(bf16[8,4,64,128]{3,2,1,0:T(8,128)(2,1)} %get-tuple-element.23), channel_id=1, source_target_pairs={{8,0},{16,8},{24,16},{9,1},{17,9},{25,17},{10,2},{18,10},{26,18},{... | collective-permute-start | bytes 1572872 | tf_op jit(solution)/shard_map/ppermute | solution.py:212
  43.7 4.0 %copy-start.2 = (bf16[8,4,64,128]{3,2,1,0:T(8,128)(2,1)}, bf16[8,4,64,128]{3,2,1,0:T(8,128)(2,1)S(1)}, u32[]{:S(2)}) copy-start(bf16[8,4,64,128]{3,2,1,0:T(8,128)(2,1)S(1)} %collective-permute-done.2.fromlow_ref) | copy-start | bytes 1572868
  47.8 0.8 copy-start.3
  52.3 13.3 %collective-permute-start.4 = (bf16[8,2,64,128]{3,2,1,0:T(8,128)(2,1)}, bf16[8,2,64,128]{3,2,1,0:T(8,128)(2,1)S(1)}, u32[]{:S(2)}, u32[]{:S(2)}) collective-permute-start(bf16[8,2,64,128]{3,2,1,0:T(8,128)(2,1)} %get-tuple-element.25), channel_id=1, source_target_pairs={{0,2},{2,4},{4,6},{1,3},{3,5},{5,7},{8,10},{10,12},{12,14},{9,11},... | collective-permute-start | bytes 786440 | tf_op jit(solution)/shard_map/ppermute | solution.py:212
  53.6 12.0 %collective-permute-start.5 = (bf16[8,2,64,128]{3,2,1,0:T(8,128)(2,1)}, bf16[8,2,64,128]{3,2,1,0:T(8,128)(2,1)S(1)}, u32[]{:S(2)}, u32[]{:S(2)}) collective-permute-start(bf16[8,2,64,128]{3,2,1,0:T(8,128)(2,1)} %get-tuple-element.26), channel_id=1, source_target_pairs={{2,0},{4,2},{6,4},{3,1},{5,3},{7,5},{10,8},{12,10},{14,12},{11,9},... | collective-permute-start | bytes 786440 | tf_op jit(solution)/shard_map/ppermute | solution.py:212
  65.6 0.7 copy-start.6
  65.6 0.8 copy-start.7
  70.4 15.2 %collective-permute-start.6 = (bf16[8,4,64,128]{3,2,1,0:T(8,128)(2,1)}, bf16[8,4,64,128]{3,2,1,0:T(8,128)(2,1)S(1)}, u32[]{:S(2)}, u32[]{:S(2)}) collective-permute-start(bf16[8,4,64,128]{3,2,1,0:T(8,128)(2,1)} %get-tuple-element.29), channel_id=1, source_target_pairs={{0,8},{8,16},{16,24},{1,9},{9,17},{17,25},{2,10},{10,18},{18,26},{... | collective-permute-start | bytes 1572872 | tf_op jit(solution)/shard_map/ppermute | solution.py:212
  73.8 15.8 %collective-permute-start.7 = (bf16[8,4,64,128]{3,2,1,0:T(8,128)(2,1)}, bf16[8,4,64,128]{3,2,1,0:T(8,128)(2,1)S(1)}, u32[]{:S(2)}, u32[]{:S(2)}) collective-permute-start(bf16[8,4,64,128]{3,2,1,0:T(8,128)(2,1)} %get-tuple-element.30), channel_id=1, source_target_pairs={{8,0},{16,8},{24,16},{9,1},{17,9},{25,17},{10,2},{18,10},{26,18},{... | collective-permute-start | bytes 1572872 | tf_op jit(solution)/shard_map/ppermute | solution.py:212
  85.6 4.0 %copy-start = (bf16[8,4,64,128]{3,2,1,0:T(8,128)(2,1)}, bf16[8,4,64,128]{3,2,1,0:T(8,128)(2,1)S(1)}, u32[]{:S(2)}) copy-start(bf16[8,4,64,128]{3,2,1,0:T(8,128)(2,1)S(1)} %collective-permute-done.6.fromlow_ref) | copy-start | bytes 1572868
  89.6 0.8 copy-start.1
